TPU v7x, 32 devices: a whole 2x2x4 slice. The times are simulated.
32 devices in a mesh: skyy: 4 (over x, core), skyx: 8 (over z, y).
Axes of the slice: x: 2, y: 2, z: 4, core: 2. Of those that a mesh axis runs over, the one named last changes fastest.
Arguments:
- tiles: bfloat16 [4, 64, 256, 256], P('skyy', 'skyx'), may hold values from -6 to 6
- coeffs: bfloat16 [4, 64, 5, 256, 256], P('skyy', 'skyx'), may hold values from -4 to 4
- weights: bfloat16 [4, 64], P('skyy', 'skyx'), may hold values from 0.25 to 4
- tile_slot: int32 [4, 64], P('skyy', 'skyx'), may hold values from 0 to 15, as said below
- slot_offset: int32 [2, 4, 128], P(None, 'skyy', 'skyx'), may hold values from -224 to 480
Outputs:
- coadd: float32 [2048, 4096], P('skyy', 'skyx')
- detection: float32 [2048, 4096], P('skyy', 'skyx')
Inputs may be any that keep to these rules, and one draw needn't show every extreme that they name: `tile_slot`: within one device the values are distinct; each device sends at most 2 tiles to one patch, and in every row of patches one patch receives 2 tiles from every device of that row.
All inputs are finite; a program needn't handle non-finite values.
Results may differ from a plain program's by a relative error of at most 0.013.
Values may be sent and summed in bfloat16 or wider, within the bound.
A program may use at most 192 MiB of HBM per device.

v0:
```python
import jax
import jax.numpy as jnp
from jax import lax
from jax.sharding import PartitionSpec as P

NB = 5
REACH = 10
CAP = 2
PATCH = 512


basis_widths = (1.0, 1.8, 2.6, 3.6, 5.0)
detect_width = 2.5


def padded(cells, sides, width):
    for axis, dim in sides:
        count = lax.axis_size(axis)
        ends = count - 1
        head = lax.slice_in_dim(cells, 0, width, axis=dim)
        tail = lax.slice_in_dim(cells, cells.shape[dim] - width, cells.shape[dim], axis=dim)
        cells = jnp.concatenate(
            [
                lax.ppermute(tail, axis, [(i, (i + 1) % count) for i in range(ends)]),
                cells,
                lax.ppermute(head, axis, [((i + 1) % count, i) for i in range(ends)]),
            ],
            axis=dim,
        )
    return cells


def band_matrices(size):
    rows = jnp.arange(size, dtype=jnp.int32)[:, None]
    cols = jnp.arange(size, dtype=jnp.int32)[None, :]
    gap = (cols - rows).astype(jnp.float32)
    inside = jnp.abs(cols - rows) <= REACH
    taps = jnp.arange(-REACH, REACH + 1).astype(jnp.float32)
    mats = []
    for width in basis_widths:
        total = jnp.sum(jnp.exp(-taps * taps / (2.0 * width * width)))
        mats.append(jnp.where(inside, jnp.exp(-gap * gap / (2.0 * width * width)) / total, 0.0))
    return jnp.stack(mats).astype(jnp.bfloat16)


def match_batch(batch_tiles, batch_coeffs, basis):
    vert = jnp.einsum(
        "bij,mjk->mbik", basis, batch_tiles, preferred_element_type=jnp.float32
    ).astype(jnp.bfloat16)
    horiz = jnp.einsum("mbik,bjk->mbij", vert, basis, preferred_element_type=jnp.float32)
    result = jnp.sum(batch_coeffs.astype(jnp.float32) * horiz, axis=1).astype(jnp.bfloat16)
    return lax.optimization_barrier(result)


def coadd_patch(matched, slot_weight, offsets, patch):
    slot_count = matched.shape[0]
    size = matched.shape[1]
    local = jnp.arange(size, dtype=jnp.int32)
    pixel = jnp.arange(patch, dtype=jnp.int32)
    row_hit = offsets[0][:, None, None] + local[None, :, None] == pixel[None, None, :]
    col_hit = offsets[1][:, None, None] + local[None, :, None] == pixel[None, None, :]
    row_place = row_hit.astype(jnp.bfloat16)
    placed = jnp.einsum("sip,sij->psj", row_place, matched, preferred_element_type=jnp.float32)
    placed = placed.astype(jnp.bfloat16).reshape(patch, slot_count * size)
    zero_weight = jnp.zeros((), jnp.bfloat16)
    col_place = jnp.where(col_hit, slot_weight[:, None, None], zero_weight).reshape(
        slot_count * size, patch
    )
    numer = jnp.dot(placed, col_place, preferred_element_type=jnp.float32)
    row_cover = jnp.any(row_hit, axis=1).astype(jnp.float32)
    col_cover = jnp.where(jnp.any(col_hit, axis=1), slot_weight[:, None].astype(jnp.float32), 0.0)
    cover = jnp.dot(
        row_cover.T, col_cover, precision=lax.Precision.HIGHEST, preferred_element_type=jnp.float32
    )
    return numer / (1.0 + cover)


def detect_kernel():
    taps = jnp.arange(-REACH, REACH + 1).astype(jnp.float32)
    kernel = jnp.exp(-taps * taps / (2.0 * detect_width * detect_width))
    return kernel / jnp.sum(kernel)


def vertical_pass(extended, out_rows):
    kernel = detect_kernel()
    vert = jnp.zeros((out_rows, extended.shape[1]), jnp.float32)
    for step in range(2 * REACH + 1):
        vert = vert + kernel[step] * extended[step : step + out_rows, :]
    return vert


def horizontal_pass(vert, out_cols):
    kernel = detect_kernel()
    result = jnp.zeros((vert.shape[0], out_cols), jnp.float32)
    for step in range(2 * REACH + 1):
        result = result + kernel[step] * vert[:, step : step + out_cols]
    return result


def body(tiles, coeffs, weights, tile_slot, slot_offset):
    count = tiles.shape[1]
    size = tiles.shape[2]
    columns = lax.axis_size("skyx")
    slots = columns * CAP
    patch = PATCH
    basis = band_matrices(size)
    own_tiles = tiles[0]
    own_coeffs = coeffs[0]
    own_weight = weights[0]
    own_slot = tile_slot[0]
    offsets = slot_offset[:, 0, :]
    send_weight = (
        jnp.zeros((slots,), jnp.bfloat16).at[own_slot].set(own_weight).reshape(columns, CAP)
    )
    grouped_tiles = own_tiles.reshape(count // CAP, CAP, size, size)
    grouped_coeffs = own_coeffs.reshape(count // CAP, CAP, NB, size, size)
    own_matched = lax.map(
        lambda pair: match_batch(pair[0], pair[1], basis), (grouped_tiles, grouped_coeffs)
    )
    own_matched = own_matched.reshape(count, size, size)
    send_matched = jnp.zeros((slots, size, size), jnp.bfloat16).at[own_slot].set(own_matched)
    send_matched = send_matched.reshape(columns, CAP, size, size)
    matched, recv_weight = (
        lax.all_to_all(send_matched, "skyx", split_axis=0, concat_axis=0, tiled=True),
        lax.all_to_all(send_weight, "skyx", split_axis=0, concat_axis=0, tiled=True),
    )
    matched = matched.reshape(slots, size, size)
    recv_weight = recv_weight.reshape(slots)
    coadd = coadd_patch(matched, recv_weight, offsets, patch)
    extended = padded(coadd.astype(jnp.bfloat16), (("skyy", 0), ("skyx", 1)), REACH).astype(
        coadd.dtype
    )
    detection = horizontal_pass(vertical_pass(extended, patch), patch)
    return (coadd, detection)


def solution(mesh):
    in_specs = (
        P("skyy", "skyx", None, None),
        P("skyy", "skyx", None, None, None),
        P("skyy", "skyx"),
        P("skyy", "skyx"),
        P(None, "skyy", "skyx"),
    )
    out_specs = (P("skyy", "skyx"), P("skyy", "skyx"))
    return jax.shard_map(body, mesh=mesh, in_specs=in_specs, out_specs=out_specs, check_vma=False)
```

profile of v0, /device:TPU:9, one launch (start us, length us, event | category | flops | bytes accessed | tf_op | source)
XLA Modules:
  0.0 142.9 jit_solution(6528796491924352530)
XLA Ops:
  1.3 0.7 scatter_custom_fusion.1
  2.0 0.7 all_to_all.12
  2.7 5.7 %all-to-all-start.1 = ((bf16[8,1,2]{2,1,0:T(2,128)(2,1)}), bf16[8,1,2]{2,1,0:T(2,128)(2,1)S(1)}, u32[]{:S(2)}, u32[]{:S(2)}) async-start(bf16[8,1,2]{2,1,0:T(2,128)(2,1)} %all_to_all.12), calls=%async_computation.1 | async-start | bytes 8192 | tf_op jit(solution)/shard_map/all_to_all | solution.py:125
  9.1 0.7 exponential_reduce_fusion.3
  11.0 0.7 exponential_reduce_fusion
  11.7 0.7 fusion.68
  12.4 1.5 %copy.14 = bf16[1,8,256,256]{2,3,1,0:T(8,128)(2,1)S(1)} copy(bf16[1,8,256,256]{3,2,1,0:T(8,128)(2,1)} %param.7) | data formatting | bytes 2097152 | tf_op args[0]
  13.9 0.8 fusion.69
  15.3 0.7 fusion.71
  16.0 0.7 fusion.72
  16.7 9.6 %while.10 = (s32[]{:T(128)}, bf16[4,2,256,256]{3,2,1,0:T(8,128)(2,1)S(1)}, bf16[4,2,5,256,256]{4,3,2,1,0:T(8,128)(2,1)}, bf16[4,2,256,256]{2,3,1,0:T(8,128)(2,1)...) while((s32[]{:T(128)}, bf16[4,2,256,256]{3,2,1,0:T(8,128)(2,1)S(1)}, ...), condition=%wide.region_7.8_spmd, body=%wide.region_5.0_spmd.sunk | while | flops 673579008 | bytes 3671113 | solution.py:117
  16.8 2.3 %fusion.95 = bf16[2,256,256]{2,1,0:T(8,128)(2,1)S(1)} fusion(bf16[5,256,256]{2,1,0:T(8,128)(2,1)S(1)} %get-tuple-element.133, bf16[4,2,256,256]{2,3,1,0:T(8,128)(2,1)S(1)} %get-tuple-element.132, s32[]{:T(128)} %get-tuple-element.123, bf16[4,2,5,256,256]{4,3,2,1,0:T(8,128)(2,1)} %get-tuple-element.131), kind=kOutput, calls=%fused_computation.3.clone.1 | convolution fusion | flops 673579008 | bytes 3146752 | tf_op jit(solution)/shard_map/while/body/eval_jaxpr/mbik,bjk->mbij/dot_general | solution.py:50
  19.2 2.3 %fusion.95 = bf16[2,256,256]{2,1,0:T(8,128)(2,1)S(1)} fusion(bf16[5,256,256]{2,1,0:T(8,128)(2,1)S(1)} %get-tuple-element.133, bf16[4,2,256,256]{2,3,1,0:T(8,128)(2,1)S(1)} %get-tuple-element.132, s32[]{:T(128)} %get-tuple-element.123, bf16[4,2,5,256,256]{4,3,2,1,0:T(8,128)(2,1)} %get-tuple-element.131), kind=kOutput, calls=%fused_computation.3.clone.1 | convolution fusion | flops 673579008 | bytes 3146752 | tf_op jit(solution)/shard_map/while/body/eval_jaxpr/mbik,bjk->mbij/dot_general | solution.py:50
  21.6 2.3 %fusion.95 = bf16[2,256,256]{2,1,0:T(8,128)(2,1)S(1)} fusion(bf16[5,256,256]{2,1,0:T(8,128)(2,1)S(1)} %get-tuple-element.133, bf16[4,2,256,256]{2,3,1,0:T(8,128)(2,1)S(1)} %get-tuple-element.132, s32[]{:T(128)} %get-tuple-element.123, bf16[4,2,5,256,256]{4,3,2,1,0:T(8,128)(2,1)} %get-tuple-element.131), kind=kOutput, calls=%fused_computation.3.clone.1 | convolution fusion | flops 673579008 | bytes 3146752 | tf_op jit(solution)/shard_map/while/body/eval_jaxpr/mbik,bjk->mbij/dot_general | solution.py:50
  23.9 2.3 %fusion.95 = bf16[2,256,256]{2,1,0:T(8,128)(2,1)S(1)} fusion(bf16[5,256,256]{2,1,0:T(8,128)(2,1)S(1)} %get-tuple-element.133, bf16[4,2,256,256]{2,3,1,0:T(8,128)(2,1)S(1)} %get-tuple-element.132, s32[]{:T(128)} %get-tuple-element.123, bf16[4,2,5,256,256]{4,3,2,1,0:T(8,128)(2,1)} %get-tuple-element.131), kind=kOutput, calls=%fused_computation.3.clone.1 | convolution fusion | flops 673579008 | bytes 3146752 | tf_op jit(solution)/shard_map/while/body/eval_jaxpr/mbik,bjk->mbij/dot_general | solution.py:50
  26.5 0.9 scatter_fusion
  27.4 2.4 %copy.16 = bf16[8,2,256,256]{2,3,1,0:T(8,128)(2,1)} copy(bf16[8,2,256,256]{3,2,1,0:T(8,128)(2,1)S(1)} %bitcast.82) | data formatting | bytes 4194304 | tf_op jit(solution)/shard_map/reshape | solution.py:122
  29.8 5.6 %all-to-all-start = ((bf16[8,2,256,256]{2,3,1,0:T(8,128)(2,1)}), bf16[8,2,256,256]{2,3,1,0:T(8,128)(2,1)S(1)}, u32[]{:S(2)}, u32[]{:S(2)}) async-start(bf16[8,2,256,256]{2,3,1,0:T(8,128)(2,1)} %copy.16), calls=%async_computation | async-start | bytes 4194304 | tf_op jit(solution)/shard_map/all_to_all | solution.py:124
  36.7 1.6 %fusion.10 = pred[16,512]{1,0:T(8,128)(4,1)S(1)} fusion(s32[16,256]{1,0:T(8,128)S(1)} %get-tuple-element.84), kind=kLoop, calls=%fused_computation.14 | loop fusion | flops 4186112 | bytes 24576 | tf_op jit(solution)/shard_map/reduce_or | solution.py:71
  38.3 1.6 %fusion.12 = pred[16,512]{1,0:T(8,128)(4,1)S(1)} fusion(s32[16,256]{1,0:T(8,128)S(1)} %get-tuple-element.85), kind=kLoop, calls=%fused_computation.17 | loop fusion | flops 4186112 | bytes 24576 | tf_op jit(solution)/shard_map/reduce_or | solution.py:70
  40.0 41.6 %all-to-all-done = bf16[8,2,256,256]{2,3,1,0:T(8,128)(2,1)S(1)} async-done(((bf16[8,2,256,256]{2,3,1,0:T(8,128)(2,1)}), bf16[8,2,256,256]{2,3,1,0:T(8,128)(2,1)S(1)}, u32[]{:S(2)}, u32[]{:S(2)}) %all-to-all-start) | async-done | bytes 2097184 | tf_op jit(solution)/shard_map/all_to_all | solution.py:124
  81.6 4.3 %fusion.22 = f32[512,512]{1,0:T(8,128)S(1)} fusion(s32[16,256]{1,0:T(8,128)S(1)} %get-tuple-element.84, bf16[16]{0:T(256)(128)(2,1)S(1)} %broadcast_in_dim.55, bf16[16,256,256]{1,2,0:T(8,128)(2,1)S(1)} %bitcast.83, s32[16,256]{1,0:T(8,128)S(1)} %get-tuple-element.85), kind=kOutput, calls=%fused_computation.26 | convolution fusion | flops 3229614080 | bytes 3178528 | tf_op jit(solution)/shard_map/dot_general | solution.py:69
  85.9 1.7 %fusion.85 = (bf16[512,512]{1,0:T(8,128)(2,1)S(1)}, f32[512,512]{1,0:T(8,128)}) fusion(f32[512,512]{1,0:T(8,128)S(1)} %fusion.22, pred[16,512]{1,0:T(8,128)(4,1)S(1)} %fusion.12, pred[16,512]{1,0:T(8,128)(4,1)S(1)} %fusion.10, f32[16]{0:T(128)S(1)} %convert_element_type.93), kind=kOutput, calls=%fused_computation.153 | convolution fusion | flops 51126272 | bytes 2637888 | tf_op jit(solution)/shard_map/dot_general | solution.py:72
  87.6 3.5 %collective-permute-start = (bf16[10,512]{1,0:T(8,128)(2,1)S(1)}, bf16[10,512]{1,0:T(8,128)(2,1)S(1)}, u32[]{:S(2)}, u32[]{:S(2)}) collective-permute-start(bf16[10,512]{1,0:T(8,128)(2,1)S(1)} %get-tuple-element.57), channel_id=1, source_target_pairs={{0,8},{8,16},{16,24},{1,9},{9,17},{17,25},{2,10},{10,18},{18,26},{... | collective-permute-start | bytes 30728 | tf_op jit(solution)/shard_map/ppermute | solution.py:24
  91.1 1.9 %collective-permute-start.1 = (bf16[10,512]{1,0:T(8,128)(2,1)S(1)}, bf16[10,512]{1,0:T(8,128)(2,1)S(1)}, u32[]{:S(2)}, u32[]{:S(2)}) collective-permute-start(bf16[10,512]{1,0:T(8,128)(2,1)S(1)} %get-tuple-element.58), channel_id=1, source_target_pairs={{8,0},{16,8},{24,16},{9,1},{17,9},{25,17},{10,2},{18,10},{26,18},{... | collective-permute-start | bytes 30728 | tf_op jit(solution)/shard_map/ppermute | solution.py:26
  93.0 0.7 fusion.83
  93.8 2.4 %collective-permute-done.1 = bf16[10,512]{1,0:T(8,128)(2,1)S(1)} collective-permute-done((bf16[10,512]{1,0:T(8,128)(2,1)S(1)}, bf16[10,512]{1,0:T(8,128)(2,1)S(1)}, u32[]{:S(2)}, u32[]{:S(2)}) %collective-permute-start.1) | collective-permute-done | bytes 10272 | tf_op jit(solution)/shard_map/ppermute | solution.py:26
  96.3 2.6 %collective-permute-start.2 = (bf16[532,10]{1,0:T(8,128)(2,1)S(1)}, bf16[532,10]{1,0:T(8,128)(2,1)S(1)}, u32[]{:S(2)}, u32[]{:S(2)}) collective-permute-start(bf16[532,10]{1,0:T(8,128)(2,1)S(1)} %get-tuple-element.55), channel_id=1, source_target_pairs={{0,1},{1,2},{2,3},{3,4},{4,5},{5,6},{6,7},{8,9},{9,10},{10,11},{11... | collective-permute-start | bytes 31928 | tf_op jit(solution)/shard_map/ppermute | solution.py:24
  98.9 4.8 %collective-permute-start.3 = (bf16[532,10]{1,0:T(8,128)(2,1)S(1)}, bf16[532,10]{1,0:T(8,128)(2,1)S(1)}, u32[]{:S(2)}, u32[]{:S(2)}) collective-permute-start(bf16[532,10]{1,0:T(8,128)(2,1)S(1)} %get-tuple-element.56), channel_id=1, source_target_pairs={{1,0},{2,1},{3,2},{4,3},{5,4},{6,5},{7,6},{9,8},{10,9},{11,10},{12... | collective-permute-start | bytes 31928 | tf_op jit(solution)/shard_map/ppermute | solution.py:26
  104.3 2.3 %collective-permute-done.3 = bf16[532,10]{1,0:T(8,128)(2,1)S(1)} collective-permute-done((bf16[532,10]{1,0:T(8,128)(2,1)S(1)}, bf16[532,10]{1,0:T(8,128)(2,1)S(1)}, u32[]{:S(2)}, u32[]{:S(2)}) %collective-permute-start.3) | collective-permute-done | bytes 10672 | tf_op jit(solution)/shard_map/ppermute | solution.py:26
  107.1 16.4 %fusion.28 = f32[512,532]{1,0:T(8,128)S(1)} fusion(f32[532,532]{1,0:T(8,128)S(1)} %maximum_convert_fusion, f32[]{:T(128)} %bitcast.40, f32[]{:T(128)} %bitcast.39, f32[]{:T(128)} %bitcast.38, f32[]{:T(128)} %bitcast.37, f32[]{:T(128)} %bitcast.36, f32[]{:T(128)} %bitcast.35, f32[]{:T(128)} %bitcast.34, f32[]{:T(128)} %bitcast.33, f32[]{:T(128)} %bitcast.32, ...), kind=kLoop, calls=%fused_computation.30 | loop fusion | flops 11167744 | bytes 23969876 | tf_op jit(solution)/shard_map/add | solution.py:88
  123.5 19.4 %fusion.48 = f32[512,512]{1,0:T(8,128)} fusion(f32[512,532]{1,0:T(8,128)S(1)} %fusion.28, f32[]{:T(128)} %bitcast.40, f32[]{:T(128)} %bitcast.39, f32[]{:T(128)} %bitcast.38, f32[]{:T(128)} %bitcast.37, f32[]{:T(128)} %bitcast.36, f32[]{:T(128)} %bitcast.35, f32[]{:T(128)} %bitcast.34, f32[]{:T(128)} %bitcast.33, f32[]{:T(128)} %bitcast.32, f32[]{:T(128)} %bitcast.31, ...), kind=kLoop, calls=%fused_computation.71 | loop fusion | flops 10747904 | bytes 23068756 | tf_op jit(solution)/shard_map/add | solution.py:96
  (27 shorter events, 6.2 us)
Async XLA Ops:
  2.7 27.1 %all-to-all-start.1 = ((bf16[8,1,2]{2,1,0:T(2,128)(2,1)}), bf16[8,1,2]{2,1,0:T(2,128)(2,1)S(1)}, u32[]{:S(2)}, u32[]{:S(2)}) async-start(bf16[8,1,2]{2,1,0:T(2,128)(2,1)} %all_to_all.12), calls=%async_computation.1 | async-start | bytes 8192 | tf_op jit(solution)/shard_map/all_to_all | solution.py:125
  29.8 6.9 %copy-start = (s32[2,1,16]{2,1,0:T(1,128)S(1)}, s32[2,1,16]{2,1,0:T(1,128)}, u32[]{:S(2)}) copy-start(s32[2,1,16]{2,1,0:T(1,128)} %param.11) | copy-start | bytes 388
  29.8 51.8 %all-to-all-start = ((bf16[8,2,256,256]{2,3,1,0:T(8,128)(2,1)}), bf16[8,2,256,256]{2,3,1,0:T(8,128)(2,1)S(1)}, u32[]{:S(2)}, u32[]{:S(2)}) async-start(bf16[8,2,256,256]{2,3,1,0:T(8,128)(2,1)} %copy.16), calls=%async_computation | async-start | bytes 4194304 | tf_op jit(solution)/shard_map/all_to_all | solution.py:124
  87.6 6.2 %collective-permute-start = (bf16[10,512]{1,0:T(8,128)(2,1)S(1)}, bf16[10,512]{1,0:T(8,128)(2,1)S(1)}, u32[]{:S(2)}, u32[]{:S(2)}) collective-permute-start(bf16[10,512]{1,0:T(8,128)(2,1)S(1)} %get-tuple-element.57), channel_id=1, source_target_pairs={{0,8},{8,16},{16,24},{1,9},{9,17},{17,25},{2,10},{10,18},{18,26},{... | collective-permute-start | bytes 30728 | tf_op jit(solution)/shard_map/ppermute | solution.py:24
  91.1 5.1 %collective-permute-start.1 = (bf16[10,512]{1,0:T(8,128)(2,1)S(1)}, bf16[10,512]{1,0:T(8,128)(2,1)S(1)}, u32[]{:S(2)}, u32[]{:S(2)}) collective-permute-start(bf16[10,512]{1,0:T(8,128)(2,1)S(1)} %get-tuple-element.58), channel_id=1, source_target_pairs={{8,0},{16,8},{24,16},{9,1},{17,9},{25,17},{10,2},{18,10},{26,18},{... | collective-permute-start | bytes 30728 | tf_op jit(solution)/shard_map/ppermute | solution.py:26
  96.3 8.1 %collective-permute-start.2 = (bf16[532,10]{1,0:T(8,128)(2,1)S(1)}, bf16[532,10]{1,0:T(8,128)(2,1)S(1)}, u32[]{:S(2)}, u32[]{:S(2)}) collective-permute-start(bf16[532,10]{1,0:T(8,128)(2,1)S(1)} %get-tuple-element.55), channel_id=1, source_target_pairs={{0,1},{1,2},{2,3},{3,4},{4,5},{5,6},{6,7},{8,9},{9,10},{10,11},{11... | collective-permute-start | bytes 31928 | tf_op jit(solution)/shard_map/ppermute | solution.py:24
  98.9 7.7 %collective-permute-start.3 = (bf16[532,10]{1,0:T(8,128)(2,1)S(1)}, bf16[532,10]{1,0:T(8,128)(2,1)S(1)}, u32[]{:S(2)}, u32[]{:S(2)}) collective-permute-start(bf16[532,10]{1,0:T(8,128)(2,1)S(1)} %get-tuple-element.56), channel_id=1, source_target_pairs={{1,0},{2,1},{3,2},{4,3},{5,4},{6,5},{7,6},{9,8},{10,9},{11,10},{12... | collective-permute-start | bytes 31928 | tf_op jit(solution)/shard_map/ppermute | solution.py:26
where the time goes:
time: 146 us; the launch traced here: 143 us
  other arithmetic  48.4 us (33%)
  waiting for transfers between devices  46.3 us (32%)
  starting transfers between devices  24.1 us (17%)
  matrix products  15.4 us (11%)
  local copies, waits for them, and re-layouts  7.93 us (5%)
    all_to_all x1, waiting for transfers between devices, body(): lax.all_to_all(send_matched, 'skyx', split_axis=0, concat_axis=0, tiled=T...  41.6 us
    add x1, other arithmetic, horizontal_pass(): result = result + kernel[step] * vert[:, step:step + out_cols]  19.4 us
    add x1, other arithmetic, vertical_pass(): vert = vert + kernel[step] * extended[step:step + out_rows, :]  16.4 us
    dot_general x4, matrix products, match_batch(): jnp.einsum('mbik,bjk->mbij', vert, basis, preferred_element_type=jnp.floa...  9.37 us
    ppermute x2, starting transfers between devices, padded(): lax.ppermute(head, axis, [((i + 1) % count, i) for i in range(ends)])  6.73 us
    ppermute x2, starting transfers between devices, padded(): lax.ppermute(tail, axis, [(i, (i + 1) % count) for i in range(ends)])  6.07 us
    all_to_all x1, starting transfers between devices, body(): lax.all_to_all(send_weight, 'skyx', split_axis=0, concat_axis=0, tiled=True)  5.72 us
    all_to_all x1, starting transfers between devices, body(): lax.all_to_all(send_matched, 'skyx', split_axis=0, concat_axis=0, tiled=T...  5.57 us
  transfers between devices with their start and end apart: 6, of which 3 were waited for; matrix products, arithmetic and copies ran while one was open for 19% of the time, Pallas kernels for 0%

commit v1 on v0

v1 whole, which is shorter than its diff:
```python
import functools

import jax
import jax.numpy as jnp
import numpy as np
from jax import lax
from jax.experimental import pallas as pl
from jax.experimental.pallas import tpu as pltpu
from jax.sharding import PartitionSpec as P

NB = 5
REACH = 10
CAP = 2
PATCH = 512
EDGE = 16
LANES = 128

basis_widths = (1.0, 1.8, 2.6, 3.6, 5.0)
detect_width = 2.5
MESH = pl.DeviceIdType.MESH


def band_matrices(size):
    rows = np.arange(size)[:, None]
    cols = np.arange(size)[None, :]
    gap = (cols - rows).astype(np.float32)
    inside = np.abs(cols - rows) <= REACH
    taps = np.arange(-REACH, REACH + 1).astype(np.float32)
    mats = []
    for width in basis_widths:
        total = np.sum(np.exp(-taps * taps / np.float32(2.0 * width * width)))
        mats.append(np.where(inside, np.exp(-gap * gap / np.float32(2.0 * width * width)) / total, 0.0))
    return np.concatenate(mats).astype(jnp.bfloat16)


def detect_matrix(positions, size):
    taps = np.arange(-REACH, REACH + 1).astype(np.float32)
    total = np.sum(np.exp(-taps * taps / np.float32(2.0 * detect_width * detect_width)))
    gap = np.asarray(positions)[:, None] - np.arange(size)[None, :]
    value = np.exp(-(gap * gap).astype(np.float32) / np.float32(2.0 * detect_width * detect_width)) / total
    return np.where(np.abs(gap) <= REACH, value, 0.0).astype(jnp.bfloat16)


def dot(a, b):
    return jnp.dot(a, b, preferred_element_type=jnp.float32)


def dot_t(a, b):
    return lax.dot_general(a, b, (((1,), (1,)), ((), ())), preferred_element_type=jnp.float32)


def dot_0(a, b):
    return lax.dot_general(a, b, (((0,), (0,)), ((), ())), preferred_element_type=jnp.float32)


def kernel(
    rows, n,
    which, wslot, offs,
    tiles_hbm, coeffs_hbm, basis, gmid, gedge, gedge_t, gcorner, pick,
    coadd_hbm, detect_hbm,
    tiles, coeffs, send, recv, wsend, wrecv, numer, result, rowcov, colcov,
    cb, vhalo, hsend, hhalo, corner, local_sem,
    send_sem, recv_sem, wsend_sem, wrecv_sem, hsend_sem, hrecv_sem,
):
    row, me = lax.axis_index("skyy"), lax.axis_index("skyx")
    size = tiles.shape[1]
    patch = numer.shape[0]
    f32, bf16 = jnp.float32, jnp.bfloat16

    load_tiles = pltpu.make_async_copy(tiles_hbm, tiles, local_sem.at[0])
    load_coeffs = pltpu.make_async_copy(coeffs_hbm, coeffs, local_sem.at[1])
    load_tiles.start()
    load_coeffs.start()

    vhalo[...] = jnp.zeros_like(vhalo)
    hhalo[...] = jnp.zeros_like(hhalo)
    corner[...] = jnp.zeros_like(corner)

    up, down, left, right = row > 0, row < rows - 1, me > 0, me < n - 1
    both = jnp.logical_and
    moves = [
        (0, up, -1, 0, lambda: cb.at[pl.ds(0, EDGE), :], lambda: vhalo.at[pl.ds(EDGE, EDGE), :]),
        (1, down, 1, 0, lambda: cb.at[pl.ds(patch - EDGE, EDGE), :], lambda: vhalo.at[pl.ds(0, EDGE), :]),
        (2, left, 0, -1, lambda: hsend.at[pl.ds(0, EDGE), :], lambda: hhalo.at[pl.ds(EDGE, EDGE), :]),
        (3, right, 0, 1, lambda: hsend.at[pl.ds(EDGE, EDGE), :], lambda: hhalo.at[pl.ds(0, EDGE), :]),
        (4, both(up, left), -1, -1, lambda: cb.at[pl.ds(0, EDGE), pl.ds(0, LANES)],
         lambda: corner.at[pl.ds(EDGE, EDGE), pl.ds(LANES, LANES)]),
        (5, both(up, right), -1, 1, lambda: cb.at[pl.ds(0, EDGE), pl.ds(patch - LANES, LANES)],
         lambda: corner.at[pl.ds(EDGE, EDGE), pl.ds(0, LANES)]),
        (6, both(down, left), 1, -1, lambda: cb.at[pl.ds(patch - EDGE, EDGE), pl.ds(0, LANES)],
         lambda: corner.at[pl.ds(0, EDGE), pl.ds(LANES, LANES)]),
        (7, both(down, right), 1, 1, lambda: cb.at[pl.ds(patch - EDGE, EDGE), pl.ds(patch - LANES, LANES)],
         lambda: corner.at[pl.ds(0, EDGE), pl.ds(0, LANES)]),
    ]
    opposite = {0: 1, 1: 0, 2: 3, 3: 2, 4: 7, 5: 6, 6: 5, 7: 4}

    barrier = pltpu.get_barrier_semaphore()

    def greet(d, carry):
        pl.semaphore_signal(barrier, inc=1, device_id={"skyx": lax.rem(me + d, n)}, device_id_type=MESH)
        return carry

    lax.fori_loop(1, n, greet, 0)
    expected = n - 1
    for index, exists, dy, dx, _, _ in moves:
        if dy != 0:
            @pl.when(exists)
            def _(dy=dy, dx=dx):
                pl.semaphore_signal(
                    barrier, inc=1, device_id={"skyy": row + dy, "skyx": me + dx}, device_id_type=MESH
                )
            expected = expected + jnp.where(exists, 1, 0)
    pl.semaphore_wait(barrier, expected)

    def weight_copy(d):
        return pltpu.make_async_remote_copy(
            src_ref=wsend.at[d], dst_ref=wrecv.at[d],
            send_sem=wsend_sem.at[d], recv_sem=wrecv_sem.at[d],
            device_id={"skyx": lax.rem(me + d, n)}, device_id_type=MESH,
        )

    line = lax.broadcasted_iota(jnp.int32, (8, LANES), 0)

    def weight_block(column):
        return jnp.where(line == 0, wslot[column * CAP], wslot[column * CAP + 1])

    def send_weight(d, carry):
        wsend[d] = weight_block(lax.rem(me + d, n))
        weight_copy(d).start()
        return carry

    wrecv[0] = weight_block(me)
    lax.fori_loop(1, n, send_weight, 0)

    def match(index):
        x = tiles[index]
        vert = dot(basis[...], x).astype(bf16)
        total = jnp.zeros((size, size), f32)
        for b in range(NB):
            part = slice(b * size, (b + 1) * size)
            total += coeffs[index, b].astype(f32) * dot(vert[part], basis[part, :])
        return total.astype(bf16)

    def tile_copy(j, d):
        return pltpu.make_async_remote_copy(
            src_ref=send.at[j], dst_ref=recv.at[j],
            send_sem=send_sem.at[j], recv_sem=recv_sem.at[j],
            device_id={"skyx": lax.rem(me + d, n)}, device_id_type=MESH,
        )

    def distance(step):
        t = step // CAP
        odd = lax.rem(t, 2)
        return n // 2 + ((t + 1) // 2) * (2 * odd - 1)

    load_tiles.wait()
    load_coeffs.wait()

    def send_one(step, carry):
        d = distance(step)
        s = lax.rem(step, CAP)
        j = d * CAP + s
        send[j] = match(which[lax.rem(me + d, n) * CAP + s])
        tile_copy(j, d).start()
        return carry

    steps = CAP * (n - 1)
    lax.fori_loop(0, steps, send_one, 0)

    def own(s, carry):
        recv[s] = match(which[me * CAP + s])
        return carry

    lax.fori_loop(0, CAP, own, 0)

    numer[...] = jnp.zeros_like(numer)

    def weight_in(d, carry):
        copy = weight_copy(d)
        copy.wait_recv()
        copy.wait_send()
        return carry

    lax.fori_loop(1, n, weight_in, 0)

    pixel = lax.broadcasted_iota(jnp.int32, (1, patch), 1)

    def place(j, d):
        s = lax.rem(j, CAP)
        slot = lax.rem(me - d + n, n) * CAP + s
        oy, ox = offs[0, slot], offs[1, slot]
        w = wrecv[d, pl.ds(s, 1), :]
        w = jnp.concatenate([w] * (patch // LANES), axis=1)
        rowcov[pl.ds(j, 1), :] = jnp.where((pixel >= oy) & (pixel < oy + size), 1.0, 0.0)
        colcov[pl.ds(j, 1), :] = jnp.where((pixel >= ox) & (pixel < ox + size), w, 0.0)
        r = lax.broadcasted_iota(jnp.int32, (patch, size), 0) - lax.broadcasted_iota(jnp.int32, (patch, size), 1)
        rowhit = jnp.where(r == oy, 1.0, 0.0).astype(bf16)
        c = lax.broadcasted_iota(jnp.int32, (size, patch), 1) - lax.broadcasted_iota(jnp.int32, (size, patch), 0)
        colhit = jnp.where(c == ox, w, 0.0).astype(bf16)
        placed = dot(rowhit, recv[j]).astype(bf16)
        numer[...] += dot(placed, colhit)

    def place_own(s, carry):
        place(s, 0)
        return carry

    lax.fori_loop(0, CAP, place_own, 0)

    def place_one(step, carry):
        d = distance(step)
        j = d * CAP + lax.rem(step, CAP)
        tile_copy(j, d).wait_recv()
        place(j, d)
        return carry

    lax.fori_loop(0, steps, place_one, 0)

    cover = dot_0(rowcov[...].astype(bf16), colcov[...].astype(bf16))
    coadd = numer[...] / (1.0 + cover)
    numer[...] = coadd
    cb[...] = coadd.astype(bf16)
    hsend[...] = dot_t(pick[...], cb[...]).astype(bf16)

    def halo_copy(move):
        index, _, dy, dx, src, dst = move
        return pltpu.make_async_remote_copy(
            src_ref=src(), dst_ref=dst(),
            send_sem=hsend_sem.at[index], recv_sem=hrecv_sem.at[index],
            device_id={"skyy": row + dy, "skyx": me + dx}, device_id_type=MESH,
        )

    for move in moves:
        @pl.when(move[1])
        def _(move=move):
            halo_copy(move).start()

    store_coadd = pltpu.make_async_copy(numer, coadd_hbm, local_sem.at[2])
    store_coadd.start()

    vert = dot(gmid[...], cb[...])

    def drain(step, carry):
        d = distance(step)
        tile_copy(d * CAP + lax.rem(step, CAP), d).wait_send()
        return carry

    lax.fori_loop(0, steps, drain, 0)

    for move in moves:
        @pl.when(moves[opposite[move[0]]][1])
        def _(move=move):
            halo_copy(move).wait_recv()

    vert = (vert + dot(gedge_t[...], vhalo[...])).astype(bf16)
    sides = dot_t(gmid[...], hhalo[...]).astype(bf16)
    ends = dot(gedge_t[...], corner[...]).astype(bf16)
    result[...] = dot(vert, gmid[...]) + dot(sides, gedge[...]) + dot(ends, gcorner[...])
    store_result = pltpu.make_async_copy(result, detect_hbm, local_sem.at[3])
    store_result.start()
    for move in moves:
        @pl.when(move[1])
        def _(move=move):
            halo_copy(move).wait_send()
    store_coadd.wait()
    store_result.wait()


def body(rows, n, tiles, coeffs, weights, tile_slot, slot_offset):
    count, size = tiles.shape[1], tiles.shape[2]
    slots = n * CAP
    patch = PATCH
    f32, bf16 = jnp.float32, jnp.bfloat16
    hits = tile_slot[0][:, None] == jnp.arange(slots, dtype=jnp.int32)[None, :]
    which = jnp.sum(jnp.where(hits, jnp.arange(count, dtype=jnp.int32)[:, None], 0), axis=0)
    wslot = jnp.sum(jnp.where(hits, weights[0].astype(f32)[:, None], 0.0), axis=0)

    basis = jnp.asarray(band_matrices(size))
    gmid = jnp.asarray(detect_matrix(np.arange(patch), patch))
    edge_at = np.concatenate([np.arange(-EDGE, 0), np.arange(patch, patch + EDGE)])
    gedge_np = detect_matrix(edge_at, patch)
    corner_at = np.concatenate([np.arange(-LANES, 0), np.arange(patch, patch + LANES)])
    gcorner = jnp.asarray(detect_matrix(corner_at, patch))
    pick_at = np.concatenate([np.arange(EDGE), np.arange(patch - EDGE, patch)])
    pick = jnp.asarray((pick_at[:, None] == np.arange(patch)[None, :]).astype(jnp.bfloat16))

    smem = pl.BlockSpec(memory_space=pltpu.SMEM)
    vmem = pl.BlockSpec(memory_space=pltpu.VMEM)
    anyspace = pl.BlockSpec(memory_space=pl.ANY)
    dma = pltpu.SemaphoreType.DMA
    return pl.pallas_call(
        functools.partial(kernel, rows, n),
        out_shape=[jax.ShapeDtypeStruct((patch, patch), f32)] * 2,
        in_specs=[smem] * 3 + [anyspace] * 2 + [vmem] * 6,
        out_specs=[anyspace] * 2,
        scratch_shapes=[
            pltpu.VMEM((count, size, size), bf16),
            pltpu.VMEM((count, NB, size, size), bf16),
            pltpu.VMEM((slots, size, size), bf16),
            pltpu.VMEM((slots, size, size), bf16),
            pltpu.VMEM((n, 8, LANES), f32),
            pltpu.VMEM((n, 8, LANES), f32),
            pltpu.VMEM((patch, patch), f32),
            pltpu.VMEM((patch, patch), f32),
            pltpu.VMEM((slots, patch), f32),
            pltpu.VMEM((slots, patch), f32),
            pltpu.VMEM((patch, patch), bf16),
            pltpu.VMEM((2 * EDGE, patch), bf16),
            pltpu.VMEM((2 * EDGE, patch), bf16),
            pltpu.VMEM((2 * EDGE, patch), bf16),
            pltpu.VMEM((2 * EDGE, 2 * LANES), bf16),
            dma((4,)),
            dma((slots,)),
            dma((slots,)),
            dma((n,)),
            dma((n,)),
            dma((8,)),
            dma((8,)),
        ],
        compiler_params=pltpu.CompilerParams(
            collective_id=0, has_side_effects=True, vmem_limit_bytes=44 * 1024 * 1024
        ),
        name="coadd",
    )(
        which, wslot, slot_offset[:, 0, :],
        tiles[0], coeffs[0], basis, gmid, jnp.asarray(gedge_np), jnp.asarray(gedge_np.T.copy()), gcorner, pick,
    )


def solution(mesh):
    in_specs = (
        P("skyy", "skyx", None, None),
        P("skyy", "skyx", None, None, None),
        P("skyy", "skyx"),
        P("skyy", "skyx"),
        P(None, "skyy", "skyx"),
    )
    out_specs = (P("skyy", "skyx"), P("skyy", "skyx"))
    return jax.shard_map(
        functools.partial(body, mesh.shape["skyy"], mesh.shape["skyx"]),
        mesh=mesh, in_specs=in_specs, out_specs=out_specs, check_vma=False,
    )
```

time: 146 us -> 76 us (0.52); the launches traced: 143 us -> 75.5 us
  Pallas kernels: 0 us -> 60.9 us
  waiting for transfers between devices: 46.3 us -> 0 us
  other arithmetic: 48.4 us -> 2.14 us
  starting transfers between devices: 24.1 us -> 0 us
  matrix products: 15.4 us -> 0 us
  local copies, waits for them, and re-layouts: 7.93 us -> 11.8 us
    pallas_call x0 -> x1, Pallas kernels: none -> 60.9 us  [body(): pl.pallas_call(functools.partial(kernel, rows, n), out_shape=[jax.ShapeDt...]
    all_to_all x2 -> x0, waiting for transfers between devices: 41.6 us -> none  [the longest x1 41.6 us: body(): lax.all_to_all(send_matched, 'skyx', split_axis=0, concat_axis=0, tiled=T...]
    add x3 -> x0, other arithmetic: 35.9 us -> none  [the longest x1 19.4 us: horizontal_pass(): result = result + kernel[step] * vert[:, step:step + out_cols]]
    dot_general x6 -> x0, matrix products: 15.4 us -> none  [the longest x4 9.37 us: match_batch(): jnp.einsum('mbik,bjk->mbij', vert, basis, preferred_element_type=jnp.floa...]
    ppermute x4 -> x0, starting transfers between devices: 12.8 us -> none  [the longest x2 6.73 us: padded(): lax.ppermute(head, axis, [((i + 1) % count, i) for i in range(ends)])]
    all_to_all x2 -> x0, starting transfers between devices: 11.3 us -> none  [the longest x1 5.72 us: body(): lax.all_to_all(send_weight, 'skyx', split_axis=0, concat_axis=0, tiled=True)]
    unnamed x3 -> x20, local copies, waits for them, and re-layouts: 1.48 us -> 11.8 us
    ppermute x4 -> x0, waiting for transfers between devices: 4.67 us -> none  [the longest x2 4.66 us: padded(): lax.ppermute(head, axis, [((i + 1) % count, i) for i in range(ends)])]
  transfers between devices with their start and end apart: 6 -> 0, of which waited for: 3 -> 0; matrix products, arithmetic and copies ran while one was open for 19% -> 0% of each run, Pallas kernels for 0% -> 0%
where the time goes in v1:
time: 76 us; the launch traced here: 75.5 us
  Pallas kernels  60.9 us (80%)
  local copies, waits for them, and re-layouts  11.8 us (16%)
  other arithmetic  2.14 us (3%)
    pallas_call x1, Pallas kernels, body(): pl.pallas_call(functools.partial(kernel, rows, n), out_shape=[jax.ShapeDt...  60.9 us
    unnamed x20, local copies, waits for them, and re-layouts  11.8 us

profile of v1, /device:TPU:9, one launch (start us, length us, event | category | flops | bytes accessed | tf_op | source)
XLA Modules:
  0.0 75.5 jit_solution(11789272127060178358)
XLA Ops:
  0.6 0.7 bitcast_convert_fusion
  1.3 0.7 select_reduce_fusion.wslot
  2.0 0.7 select_reduce_fusion.1.which
  2.8 0.0 copy-start
  2.8 2.5 %copy-done = bf16[1,8,5,256,256]{4,3,2,1,0:T(8,128)(2,1)S(1)} copy-done((bf16[1,8,5,256,256]{4,3,2,1,0:T(8,128)(2,1)S(1)}, bf16[1,8,5,256,256]{4,3,2,1,0:T(8,128)(2,1)}, u32[]{:S(2)}) %copy-start) | copy-done | bytes 5242904
  5.3 0.0 copy-start.1
  5.3 1.2 %copy-done.1 = bf16[1,8,256,256]{3,2,1,0:T(8,128)(2,1)S(1)} copy-done((bf16[1,8,256,256]{3,2,1,0:T(8,128)(2,1)S(1)}, bf16[1,8,256,256]{3,2,1,0:T(8,128)(2,1)}, u32[]{:S(2)}) %copy-start.1) | copy-done | bytes 1048600
  6.5 0.0 copy-start.2
  6.5 1.1 %copy-done.2 = bf16[1280,256]{1,0:T(8,128)(2,1)S(1)} copy-done((bf16[1280,256]{1,0:T(8,128)(2,1)S(1)}, bf16[1280,256]{1,0:T(8,128)(2,1)}, u32[]{:S(2)}) %copy-start.2) | copy-done | bytes 655384
  7.6 0.0 copy-start.3
  7.6 1.0 %copy-done.3 = bf16[512,512]{1,0:T(8,128)(2,1)S(1)} copy-done((bf16[512,512]{1,0:T(8,128)(2,1)S(1)}, bf16[512,512]{1,0:T(8,128)(2,1)}, u32[]{:S(2)}) %copy-start.3) | copy-done | bytes 524312
  8.6 0.0 copy-start.4
  8.6 0.9 %copy-done.4 = bf16[256,512]{1,0:T(8,128)(2,1)S(1)} copy-done((bf16[256,512]{1,0:T(8,128)(2,1)S(1)}, bf16[256,512]{1,0:T(8,128)(2,1)}, u32[]{:S(2)}) %copy-start.4) | copy-done | bytes 262168
  9.6 0.0 copy-start.5
  9.6 0.9 %copy-done.5 = bf16[512,32]{1,0:T(8,128)(2,1)S(1)} copy-done((bf16[512,32]{1,0:T(8,128)(2,1)S(1)}, bf16[512,32]{1,0:T(8,128)(2,1)}, u32[]{:S(2)}) %copy-start.5) | copy-done | bytes 32792
  10.5 0.0 copy-start.6
  10.5 0.8 %copy-done.6 = bf16[32,512]{1,0:T(8,128)(2,1)S(1)} copy-done((bf16[32,512]{1,0:T(8,128)(2,1)S(1)}, bf16[32,512]{1,0:T(8,128)(2,1)}, u32[]{:S(2)}) %copy-start.6) | copy-done | bytes 32792
  11.2 0.0 copy-start.7
  11.2 0.8 %copy-done.7 = bf16[32,512]{1,0:T(8,128)(2,1)S(1)} copy-done((bf16[32,512]{1,0:T(8,128)(2,1)S(1)}, bf16[32,512]{1,0:T(8,128)(2,1)}, u32[]{:S(2)}) %copy-start.7) | copy-done | bytes 32792
  12.0 0.0 copy-start.8
  12.0 0.7 copy-done.8
  12.7 60.9 %coadd.1 = (f32[512,512]{1,0:T(8,128)S(1)}, f32[512,512]{1,0:T(8,128)S(1)}) custom-call(s32[16]{0:T(128)S(1)} %select_reduce_fusion.1.which, f32[16]{0:T(128)S(1)} %select_reduce_fusion.wslot, s32[2,16]{1,0:T(2,128)S(1)} %bitcast.9, bf16[8,256,256]{2,1,0:T(8,128)(2,1)S(1)} %bitcast.8, bf16[8,5,256,256]{3,2,1,0:T(8,128)(2,1)S(1)} %bitcast.7, ...), custom_call_target="tpu_custom_call" | custom-call | tf_op jit(solution)/shard_map/coadd/pallas_call | solution.py:290
  73.6 1.0 %copy.15 = f32[512,512]{1,0:T(8,128)} copy(f32[512,512]{1,0:T(8,128)S(1)} %get-tuple-element.4) | data formatting | bytes 2097152
  74.5 1.0 %copy.16 = f32[512,512]{1,0:T(8,128)} copy(f32[512,512]{1,0:T(8,128)S(1)} %get-tuple-element.5) | data formatting | bytes 2097152
Async XLA Ops:
  2.8 2.5 %copy-start = (bf16[1,8,5,256,256]{4,3,2,1,0:T(8,128)(2,1)S(1)}, bf16[1,8,5,256,256]{4,3,2,1,0:T(8,128)(2,1)}, u32[]{:S(2)}) copy-start(bf16[1,8,5,256,256]{4,3,2,1,0:T(8,128)(2,1)} %param.12) | copy-start | bytes 15728644
  5.3 1.2 %copy-start.1 = (bf16[1,8,256,256]{3,2,1,0:T(8,128)(2,1)S(1)}, bf16[1,8,256,256]{3,2,1,0:T(8,128)(2,1)}, u32[]{:S(2)}) copy-start(bf16[1,8,256,256]{3,2,1,0:T(8,128)(2,1)} %param.11) | copy-start | bytes 3145732
  6.5 1.1 %copy-start.2 = (bf16[1280,256]{1,0:T(8,128)(2,1)S(1)}, bf16[1280,256]{1,0:T(8,128)(2,1)}, u32[]{:S(2)}) copy-start(bf16[1280,256]{1,0:T(8,128)(2,1)} %constant.16.clone.basis) | copy-start | bytes 1966084
  7.6 1.0 %copy-start.3 = (bf16[512,512]{1,0:T(8,128)(2,1)S(1)}, bf16[512,512]{1,0:T(8,128)(2,1)}, u32[]{:S(2)}) copy-start(bf16[512,512]{1,0:T(8,128)(2,1)} %constant.17.clone.gmid) | copy-start | bytes 1572868
  8.6 0.9 %copy-start.4 = (bf16[256,512]{1,0:T(8,128)(2,1)S(1)}, bf16[256,512]{1,0:T(8,128)(2,1)}, u32[]{:S(2)}) copy-start(bf16[256,512]{1,0:T(8,128)(2,1)} %constant.18.clone.gcorner) | copy-start | bytes 786436
  9.6 0.9 %copy-start.5 = (bf16[512,32]{1,0:T(8,128)(2,1)S(1)}, bf16[512,32]{1,0:T(8,128)(2,1)}, u32[]{:S(2)}) copy-start(bf16[512,32]{1,0:T(8,128)(2,1)} %constant.21.clone.gedge_t) | copy-start | bytes 98308
  10.5 0.8 %copy-start.6 = (bf16[32,512]{1,0:T(8,128)(2,1)S(1)}, bf16[32,512]{1,0:T(8,128)(2,1)}, u32[]{:S(2)}) copy-start(bf16[32,512]{1,0:T(8,128)(2,1)} %constant.20.clone.gedge) | copy-start | bytes 98308
  11.2 0.8 %copy-start.7 = (bf16[32,512]{1,0:T(8,128)(2,1)S(1)}, bf16[32,512]{1,0:T(8,128)(2,1)}, u32[]{:S(2)}) copy-start(bf16[32,512]{1,0:T(8,128)(2,1)} %constant.19.clone.pick) | copy-start | bytes 98308
  12.0 0.7 copy-start.8

commit v2 on v1

--- a/solution.py
+++ b/solution.py
@@ -14,6 +14,7 @@
 PATCH = 512
 EDGE = 16
 LANES = 128
+VMEM_LIMIT = 63 * 1024 * 1024
 
 basis_widths = (1.0, 1.8, 2.6, 3.6, 5.0)
 detect_width = 2.5
@@ -55,10 +56,10 @@
 
 def kernel(
     rows, n,
-    which, wslot, offs,
-    tiles_hbm, coeffs_hbm, basis, gmid, gedge, gedge_t, gcorner, pick,
+    slot_at, offs, slot_row, weight_row,
+    tiles_hbm, coeffs_hbm, basis_hbm, bands_hbm,
     coadd_hbm, detect_hbm,
-    tiles, coeffs, send, recv, wsend, wrecv, numer, result, rowcov, colcov,
+    tiles, coeffs, basis, bands, send, recv, wsend, wrecv, numer, result, rowcov, colcov,
     cb, vhalo, hsend, hhalo, corner, local_sem,
     send_sem, recv_sem, wsend_sem, wrecv_sem, hsend_sem, hrecv_sem,
 ):
@@ -69,8 +70,16 @@
 
     load_tiles = pltpu.make_async_copy(tiles_hbm, tiles, local_sem.at[0])
     load_coeffs = pltpu.make_async_copy(coeffs_hbm, coeffs, local_sem.at[1])
+    load_basis = pltpu.make_async_copy(basis_hbm, basis, local_sem.at[4])
+    load_bands = pltpu.make_async_copy(bands_hbm, bands, local_sem.at[5])
     load_tiles.start()
+    load_basis.start()
     load_coeffs.start()
+    load_bands.start()
+    gmid = bands.at[pl.ds(0, patch), :]
+    gcorner = bands.at[pl.ds(patch, 2 * LANES), :]
+    gedge = bands.at[pl.ds(patch + 2 * LANES, 2 * EDGE), :]
+    pick = bands.at[pl.ds(patch + 2 * LANES + 2 * EDGE, 2 * EDGE), :]
 
     vhalo[...] = jnp.zeros_like(vhalo)
     hhalo[...] = jnp.zeros_like(hhalo)
@@ -121,8 +130,20 @@
 
     line = lax.broadcasted_iota(jnp.int32, (8, LANES), 0)
 
+    weight_of = weight_row[...].astype(f32)
+    count = tiles.shape[0]
+
+    def slot_weight(slot):
+        return jnp.sum(jnp.where(slot_row[...] == slot, weight_of, 0.0), axis=1, keepdims=True)
+
     def weight_block(column):
-        return jnp.where(line == 0, wslot[column * CAP], wslot[column * CAP + 1])
+        return jnp.where(line == 0, slot_weight(column * CAP), slot_weight(column * CAP + 1))
+
+    def which(slot):
+        index = jnp.int32(0)
+        for m in range(count):
+            index = jnp.where(slot_at[0, m] == slot, m, index)
+        return index
 
     def send_weight(d, carry):
         wsend[d] = weight_block(lax.rem(me + d, n))
@@ -154,13 +175,14 @@
         return n // 2 + ((t + 1) // 2) * (2 * odd - 1)
 
     load_tiles.wait()
+    load_basis.wait()
     load_coeffs.wait()
 
     def send_one(step, carry):
         d = distance(step)
         s = lax.rem(step, CAP)
         j = d * CAP + s
-        send[j] = match(which[lax.rem(me + d, n) * CAP + s])
+        send[j] = match(which(lax.rem(me + d, n) * CAP + s))
         tile_copy(j, d).start()
         return carry
 
@@ -168,7 +190,7 @@
     lax.fori_loop(0, steps, send_one, 0)
 
     def own(s, carry):
-        recv[s] = match(which[me * CAP + s])
+        recv[s] = match(which(me * CAP + s))
         return carry
 
     lax.fori_loop(0, CAP, own, 0)
@@ -188,7 +210,7 @@
     def place(j, d):
         s = lax.rem(j, CAP)
         slot = lax.rem(me - d + n, n) * CAP + s
-        oy, ox = offs[0, slot], offs[1, slot]
+        oy, ox = offs[0, 0, slot], offs[1, 0, slot]
         w = wrecv[d, pl.ds(s, 1), :]
         w = jnp.concatenate([w] * (patch // LANES), axis=1)
         rowcov[pl.ds(j, 1), :] = jnp.where((pixel >= oy) & (pixel < oy + size), 1.0, 0.0)
@@ -215,6 +237,7 @@
 
     lax.fori_loop(0, steps, place_one, 0)
 
+    load_bands.wait()
     cover = dot_0(rowcov[...].astype(bf16), colcov[...].astype(bf16))
     coadd = numer[...] / (1.0 + cover)
     numer[...] = coadd
@@ -251,9 +274,9 @@
         def _(move=move):
             halo_copy(move).wait_recv()
 
-    vert = (vert + dot(gedge_t[...], vhalo[...])).astype(bf16)
+    vert = (vert + dot_0(gedge[...], vhalo[...])).astype(bf16)
     sides = dot_t(gmid[...], hhalo[...]).astype(bf16)
-    ends = dot(gedge_t[...], corner[...]).astype(bf16)
+    ends = dot_0(gedge[...], corner[...]).astype(bf16)
     result[...] = dot(vert, gmid[...]) + dot(sides, gedge[...]) + dot(ends, gcorner[...])
     store_result = pltpu.make_async_copy(result, detect_hbm, local_sem.at[3])
     store_result.start()
@@ -270,18 +293,14 @@
     slots = n * CAP
     patch = PATCH
     f32, bf16 = jnp.float32, jnp.bfloat16
-    hits = tile_slot[0][:, None] == jnp.arange(slots, dtype=jnp.int32)[None, :]
-    which = jnp.sum(jnp.where(hits, jnp.arange(count, dtype=jnp.int32)[:, None], 0), axis=0)
-    wslot = jnp.sum(jnp.where(hits, weights[0].astype(f32)[:, None], 0.0), axis=0)
-
     basis = jnp.asarray(band_matrices(size))
-    gmid = jnp.asarray(detect_matrix(np.arange(patch), patch))
     edge_at = np.concatenate([np.arange(-EDGE, 0), np.arange(patch, patch + EDGE)])
-    gedge_np = detect_matrix(edge_at, patch)
     corner_at = np.concatenate([np.arange(-LANES, 0), np.arange(patch, patch + LANES)])
-    gcorner = jnp.asarray(detect_matrix(corner_at, patch))
     pick_at = np.concatenate([np.arange(EDGE), np.arange(patch - EDGE, patch)])
-    pick = jnp.asarray((pick_at[:, None] == np.arange(patch)[None, :]).astype(jnp.bfloat16))
+    pick = (pick_at[:, None] == np.arange(patch)[None, :]).astype(jnp.bfloat16)
+    positions = np.concatenate([np.arange(patch), corner_at, edge_at])
+    bands_np = np.concatenate([detect_matrix(positions, patch), pick])
+    bands = jnp.asarray(bands_np)
 
     smem = pl.BlockSpec(memory_space=pltpu.SMEM)
     vmem = pl.BlockSpec(memory_space=pltpu.VMEM)
@@ -290,11 +309,13 @@
     return pl.pallas_call(
         functools.partial(kernel, rows, n),
         out_shape=[jax.ShapeDtypeStruct((patch, patch), f32)] * 2,
-        in_specs=[smem] * 3 + [anyspace] * 2 + [vmem] * 6,
+        in_specs=[smem] * 2 + [vmem] * 2 + [anyspace] * 4,
         out_specs=[anyspace] * 2,
         scratch_shapes=[
             pltpu.VMEM((count, size, size), bf16),
             pltpu.VMEM((count, NB, size, size), bf16),
+            pltpu.VMEM((NB * size, size), bf16),
+            pltpu.VMEM(bands_np.shape, bf16),
             pltpu.VMEM((slots, size, size), bf16),
             pltpu.VMEM((slots, size, size), bf16),
             pltpu.VMEM((n, 8, LANES), f32),
@@ -308,7 +329,7 @@
             pltpu.VMEM((2 * EDGE, patch), bf16),
             pltpu.VMEM((2 * EDGE, patch), bf16),
             pltpu.VMEM((2 * EDGE, 2 * LANES), bf16),
-            dma((4,)),
+            dma((6,)),
             dma((slots,)),
             dma((slots,)),
             dma((n,)),
@@ -317,12 +338,11 @@
             dma((8,)),
         ],
         compiler_params=pltpu.CompilerParams(
-            collective_id=0, has_side_effects=True, vmem_limit_bytes=44 * 1024 * 1024
+            collective_id=0, has_side_effects=True, vmem_limit_bytes=VMEM_LIMIT
         ),
         name="coadd",
     )(
-        which, wslot, slot_offset[:, 0, :],
-        tiles[0], coeffs[0], basis, gmid, jnp.asarray(gedge_np), jnp.asarray(gedge_np.T.copy()), gcorner, pick,
+        tile_slot, slot_offset, tile_slot, weights, tiles[0], coeffs[0], basis, bands,
     )
 
 

time: 76 us -> 67.9 us (0.89)
  local copies, waits for them, and re-layouts: 11.8 us -> 4.52 us
  other arithmetic: 2.14 us -> 0 us
  Pallas kernels: 60.9 us -> 62.5 us
    unnamed x20 -> x2, local copies, waits for them, and re-layouts: 11.8 us -> 4.52 us
    pallas_call x1, Pallas kernels: 60.9 us -> 62.5 us  [body(): pl.pallas_call(functools.partial(kernel, rows, n), out_shape=[jax.ShapeDt...]
    reduce_sum x2 -> x0, other arithmetic: 1.48 us -> none  [the longest x1 0.74 us: body(): jnp.sum(jnp.where(hits, weights[0].astype(f32)[:, None], 0.0), axis=0)]
where the time goes in v2:
time: 67.9 us; the launch traced here: 67.7 us
  Pallas kernels  62.5 us (92%)
  local copies, waits for them, and re-layouts  4.52 us (7%)
    pallas_call x1, Pallas kernels, body(): pl.pallas_call(functools.partial(kernel, rows, n), out_shape=[jax.ShapeDt...  62.5 us
    unnamed x2, local copies, waits for them, and re-layouts  4.52 us

profile of v2, /device:TPU:9, one launch (start us, length us, event | category | flops | bytes accessed | tf_op | source)
XLA Modules:
  0.0 67.7 jit_solution(17535161830575687117)
XLA Ops:
  0.6 62.5 %coadd.1 = (f32[512,512]{1,0:T(8,128)}, f32[512,512]{1,0:T(8,128)}) custom-call(s32[1,8]{1,0:T(1,128)} %slot_row.1, s32[2,1,16]{2,1,0:T(1,128)} %offs.1, s32[1,8]{1,0:T(1,128)} %slot_row.1, bf16[1,8]{1,0:T(2,128)(2,1)} %weight_row.1, bf16[8,256,256]{2,1,0:T(8,128)(2,1)} %bitcast.3, bf16[8,5,256,256]{3,2,1,0:T(8,128)(2,1)} %bitcast.2, ...), custom_call_target="tpu_custom_call" | custom-call | tf_op jit(solution)/shard_map/coadd/pallas_call | solution.py:309
  63.2 2.3 %copy.11 = f32[512,512]{1,0:T(8,128)} copy(f32[512,512]{1,0:T(8,128)} %get-tuple-element.4) | data formatting | bytes 2097152
  65.5 2.3 %copy.12 = f32[512,512]{1,0:T(8,128)} copy(f32[512,512]{1,0:T(8,128)} %get-tuple-element.5) | data formatting | bytes 2097152

commit v3 on v2

--- a/solution.py
+++ b/solution.py
@@ -59,9 +59,11 @@
     slot_at, offs, slot_row, weight_row,
     tiles_hbm, coeffs_hbm, basis_hbm, bands_hbm,
     coadd_hbm, detect_hbm,
-    tiles, coeffs, basis, bands, send, recv, wsend, wrecv, numer, result, rowcov, colcov,
+    tiles, coeffs, basis, bands, send_far, recv_far, send_near, recv_near, wsend, wrecv,
+    osend, orecv, numer, inverse, result, part_out, part_in, rowcov, colcov,
     cb, vhalo, hsend, hhalo, corner, local_sem,
-    send_sem, recv_sem, wsend_sem, wrecv_sem, hsend_sem, hrecv_sem,
+    far_send_sem, far_recv_sem, near_send_sem, near_recv_sem, wsend_sem, wrecv_sem,
+    osend_sem, orecv_sem, part_send_sem, part_recv_sem, hsend_sem, hrecv_sem,
 ):
     row, me = lax.axis_index("skyy"), lax.axis_index("skyx")
     size = tiles.shape[1]
@@ -87,6 +89,11 @@
 
     up, down, left, right = row > 0, row < rows - 1, me > 0, me < n - 1
     both = jnp.logical_and
+    span, width = n // 2, n // 4
+    half = me // span
+    local = me - half * span
+    column = lax.rem(me, width)
+    inner = me // width == 1 + half
     moves = [
         (0, up, -1, 0, lambda: cb.at[pl.ds(0, EDGE), :], lambda: vhalo.at[pl.ds(EDGE, EDGE), :]),
         (1, down, 1, 0, lambda: cb.at[pl.ds(patch - EDGE, EDGE), :], lambda: vhalo.at[pl.ds(0, EDGE), :]),
@@ -136,8 +143,32 @@
     def slot_weight(slot):
         return jnp.sum(jnp.where(slot_row[...] == slot, weight_of, 0.0), axis=1, keepdims=True)
 
-    def weight_block(column):
-        return jnp.where(line == 0, slot_weight(column * CAP), slot_weight(column * CAP + 1))
+    def far_patch(side, p, at):
+        return ((3 - p) - side * (3 - 2 * p)) * width + at
+
+    def weight_block(dest):
+        side, at = dest // span, lax.rem(dest, width)
+        block = jnp.zeros((8, LANES), f32)
+        for p, patch_at in enumerate((dest, far_patch(side, 0, at), far_patch(side, 1, at))):
+            for s in range(CAP):
+                block = jnp.where(line == p * CAP + s, slot_weight(patch_at * CAP + s), block)
+        return block
+
+    def write_offset(j, carry):
+        osend[pl.ds(2 * j, 1), :] = jnp.full((1, LANES), offs[0, 0, j], jnp.int32)
+        osend[pl.ds(2 * j + 1, 1), :] = jnp.full((1, LANES), offs[1, 0, j], jnp.int32)
+        return carry
+
+    def offset_copy(p):
+        return pltpu.make_async_remote_copy(
+            src_ref=osend, dst_ref=orecv.at[p],
+            send_sem=osend_sem.at[0], recv_sem=orecv_sem.at[p],
+            device_id={"skyx": (2 - half) * width + column}, device_id_type=MESH,
+        )
+
+    my_kind = jnp.where(inner, 1, 0)
+    lax.fori_loop(0, n * CAP, write_offset, 0)
+    offset_copy(my_kind).start()
 
     def which(slot):
         index = jnp.int32(0)
@@ -162,35 +193,77 @@
             total += coeffs[index, b].astype(f32) * dot(vert[part], basis[part, :])
         return total.astype(bf16)
 
-    def tile_copy(j, d):
+    def far_slot(p, sender, s):
+        return (p * span + sender) * CAP + s
+
+    def far_copy(p, at, s, sender):
+        out = (p * width + at) * CAP + s
+        slot = far_slot(p, sender, s)
         return pltpu.make_async_remote_copy(
-            src_ref=send.at[j], dst_ref=recv.at[j],
-            send_sem=send_sem.at[j], recv_sem=recv_sem.at[j],
-            device_id={"skyx": lax.rem(me + d, n)}, device_id_type=MESH,
-        )
-
-    def distance(step):
+            src_ref=send_far.at[out], dst_ref=recv_far.at[slot],
+            send_sem=far_send_sem.at[out], recv_sem=far_recv_sem.at[slot],
+            device_id={"skyx": (1 + half) * width + at}, device_id_type=MESH,
+        )
+
+    def near_copy(dest, s, sender):
+        return pltpu.make_async_remote_copy(
+            src_ref=send_near.at[dest * CAP + s], dst_ref=recv_near.at[sender * CAP + s],
+            send_sem=near_send_sem.at[dest * CAP + s], recv_sem=near_recv_sem.at[sender * CAP + s],
+            device_id={"skyx": half * span + dest}, device_id_type=MESH,
+        )
+
+    def part_copy(p):
+        return pltpu.make_async_remote_copy(
+            src_ref=part_out.at[p], dst_ref=part_in,
+            send_sem=part_send_sem.at[p], recv_sem=part_recv_sem.at[0],
+            device_id={"skyx": far_patch(half, p, column)}, device_id_type=MESH,
+        )
+
+    def far_step(step):
+        p = step // (width * CAP)
+        at = lax.rem(column + lax.rem(step // CAP, width), width)
+        mine = both(inner, at == column)
+        return p, at, lax.rem(step, CAP), mine
+
+    def near_step(step):
         t = step // CAP
-        odd = lax.rem(t, 2)
-        return n // 2 + ((t + 1) // 2) * (2 * odd - 1)
+        d = span // 2 + ((t + 1) // 2) * (2 * lax.rem(t, 2) - 1)
+        return d, lax.rem(step, CAP)
+
+    far_steps, near_steps = 2 * width * CAP, CAP * (span - 1)
 
     load_tiles.wait()
     load_basis.wait()
     load_coeffs.wait()
 
-    def send_one(step, carry):
-        d = distance(step)
-        s = lax.rem(step, CAP)
-        j = d * CAP + s
-        send[j] = match(which(lax.rem(me + d, n) * CAP + s))
-        tile_copy(j, d).start()
-        return carry
-
-    steps = CAP * (n - 1)
-    lax.fori_loop(0, steps, send_one, 0)
+    def send_one_far(step, carry):
+        p, at, s, mine = far_step(step)
+        tile = match(which(far_patch(half, p, at) * CAP + s))
+
+        @pl.when(mine)
+        def _():
+            recv_far[far_slot(p, local, s)] = tile
+
+        @pl.when(jnp.logical_not(mine))
+        def _():
+            send_far[(p * width + at) * CAP + s] = tile
+            far_copy(p, at, s, local).start()
+
+        return carry
+
+    lax.fori_loop(0, far_steps, send_one_far, 0)
+
+    def send_one_near(step, carry):
+        d, s = near_step(step)
+        dest = lax.rem(local + d, span)
+        send_near[dest * CAP + s] = match(which((half * span + dest) * CAP + s))
+        near_copy(dest, s, local).start()
+        return carry
+
+    lax.fori_loop(0, near_steps, send_one_near, 0)
 
     def own(s, carry):
-        recv[s] = match(which(me * CAP + s))
+        recv_near[local * CAP + s] = match(which(me * CAP + s))
         return carry
 
     lax.fori_loop(0, CAP, own, 0)
@@ -207,39 +280,83 @@
 
     pixel = lax.broadcasted_iota(jnp.int32, (1, patch), 1)
 
-    def place(j, d):
-        s = lax.rem(j, CAP)
-        slot = lax.rem(me - d + n, n) * CAP + s
-        oy, ox = offs[0, 0, slot], offs[1, 0, slot]
-        w = wrecv[d, pl.ds(s, 1), :]
-        w = jnp.concatenate([w] * (patch // LANES), axis=1)
+    def wide(line_of, size):
+        return jnp.concatenate([line_of] * (size // LANES), axis=1)
+
+    def weight_at(sender, kind, s):
+        return wrecv[lax.rem(me - sender + n, n), pl.ds(kind * CAP + s, 1), :]
+
+    def cover_one(j, carry):
+        oy, ox = offs[0, 0, j], offs[1, 0, j]
+        w = wide(weight_at(j // CAP, 0, lax.rem(j, CAP)), patch)
         rowcov[pl.ds(j, 1), :] = jnp.where((pixel >= oy) & (pixel < oy + size), 1.0, 0.0)
         colcov[pl.ds(j, 1), :] = jnp.where((pixel >= ox) & (pixel < ox + size), w, 0.0)
+        return carry
+
+    lax.fori_loop(0, n * CAP, cover_one, 0)
+    cover = dot_0(rowcov[...].astype(bf16), colcov[...].astype(bf16))
+    inverse[...] = 1.0 / (1.0 + cover)
+
+    def place(total, tile, oy, ox, w):
         r = lax.broadcasted_iota(jnp.int32, (patch, size), 0) - lax.broadcasted_iota(jnp.int32, (patch, size), 1)
-        rowhit = jnp.where(r == oy, 1.0, 0.0).astype(bf16)
+        rowhit = jnp.where(r == wide(oy, size), 1.0, 0.0).astype(bf16)
         c = lax.broadcasted_iota(jnp.int32, (size, patch), 1) - lax.broadcasted_iota(jnp.int32, (size, patch), 0)
-        colhit = jnp.where(c == ox, w, 0.0).astype(bf16)
-        placed = dot(rowhit, recv[j]).astype(bf16)
-        numer[...] += dot(placed, colhit)
-
-    def place_own(s, carry):
-        place(s, 0)
-        return carry
-
-    lax.fori_loop(0, CAP, place_own, 0)
-
-    def place_one(step, carry):
-        d = distance(step)
-        j = d * CAP + lax.rem(step, CAP)
-        tile_copy(j, d).wait_recv()
-        place(j, d)
-        return carry
-
-    lax.fori_loop(0, steps, place_one, 0)
-
+        colhit = jnp.where(c == wide(ox, patch), wide(w, patch), 0.0).astype(bf16)
+        placed = dot(rowhit, tile).astype(bf16)
+        total[...] += dot(placed, colhit)
+
+    @pl.when(inner)
+    def _():
+        offset_copy(0).wait_recv()
+        offset_copy(1).wait_recv()
+
+        def sum_far(p, carry):
+            result[...] = jnp.zeros_like(result)
+
+            def add_far(step, carry):
+                sender = lax.rem(local + step // CAP, span)
+                s = lax.rem(step, CAP)
+
+                @pl.when(sender != local)
+                def _():
+                    far_copy(p, column, s, sender).wait_recv()
+
+                whole = half * span + sender
+                at = 2 * (whole * CAP + s)
+                place(
+                    result, recv_far[far_slot(p, sender, s)],
+                    orecv[p, pl.ds(at, 1), :], orecv[p, pl.ds(at + 1, 1), :],
+                    weight_at(whole, 1 + p, s),
+                )
+                return carry
+
+            lax.fori_loop(0, span * CAP, add_far, 0)
+            part_out[p] = result[...].astype(bf16)
+            part_copy(p).start()
+            return carry
+
+        lax.fori_loop(0, 2, sum_far, 0)
+
+    def add_near(step, carry):
+        sender = lax.rem(local + step // CAP, span)
+        s = lax.rem(step, CAP)
+
+        @pl.when(sender != local)
+        def _():
+            near_copy(local, s, sender).wait_recv()
+
+        whole = half * span + sender
+        at = 2 * (whole * CAP + s)
+        place(
+            numer, recv_near[sender * CAP + s],
+            osend[pl.ds(at, 1), :], osend[pl.ds(at + 1, 1), :], weight_at(whole, 0, s),
+        )
+        return carry
+
+    lax.fori_loop(0, span * CAP, add_near, 0)
+    part_copy(0).wait_recv()
     load_bands.wait()
-    cover = dot_0(rowcov[...].astype(bf16), colcov[...].astype(bf16))
-    coadd = numer[...] / (1.0 + cover)
+    coadd = (numer[...] + part_in[...].astype(f32)) * inverse[...]
     numer[...] = coadd
     cb[...] = coadd.astype(bf16)
     hsend[...] = dot_t(pick[...], cb[...]).astype(bf16)
@@ -262,12 +379,28 @@
 
     vert = dot(gmid[...], cb[...])
 
-    def drain(step, carry):
-        d = distance(step)
-        tile_copy(d * CAP + lax.rem(step, CAP), d).wait_send()
-        return carry
-
-    lax.fori_loop(0, steps, drain, 0)
+    def drain_far(step, carry):
+        p, at, s, mine = far_step(step)
+
+        @pl.when(jnp.logical_not(mine))
+        def _():
+            far_copy(p, at, s, local).wait_send()
+
+        return carry
+
+    def drain_near(step, carry):
+        d, s = near_step(step)
+        near_copy(lax.rem(local + d, span), s, local).wait_send()
+        return carry
+
+    lax.fori_loop(0, far_steps, drain_far, 0)
+    lax.fori_loop(0, near_steps, drain_near, 0)
+    offset_copy(my_kind).wait_send()
+
+    @pl.when(inner)
+    def _():
+        part_copy(0).wait_send()
+        part_copy(1).wait_send()
 
     for move in moves:
         @pl.when(moves[opposite[move[0]]][1])
@@ -316,12 +449,19 @@
             pltpu.VMEM((count, NB, size, size), bf16),
             pltpu.VMEM((NB * size, size), bf16),
             pltpu.VMEM(bands_np.shape, bf16),
+            pltpu.VMEM((slots // 2, size, size), bf16),
             pltpu.VMEM((slots, size, size), bf16),
-            pltpu.VMEM((slots, size, size), bf16),
+            pltpu.VMEM((slots // 2, size, size), bf16),
+            pltpu.VMEM((slots // 2, size, size), bf16),
             pltpu.VMEM((n, 8, LANES), f32),
             pltpu.VMEM((n, 8, LANES), f32),
+            pltpu.VMEM((2 * slots, LANES), jnp.int32),
+            pltpu.VMEM((2, 2 * slots, LANES), jnp.int32),
             pltpu.VMEM((patch, patch), f32),
             pltpu.VMEM((patch, patch), f32),
+            pltpu.VMEM((patch, patch), f32),
+            pltpu.VMEM((2, patch, patch), bf16),
+            pltpu.VMEM((patch, patch), bf16),
             pltpu.VMEM((slots, patch), f32),
             pltpu.VMEM((slots, patch), f32),
             pltpu.VMEM((patch, patch), bf16),
@@ -330,10 +470,16 @@
             pltpu.VMEM((2 * EDGE, patch), bf16),
             pltpu.VMEM((2 * EDGE, 2 * LANES), bf16),
             dma((6,)),
+            dma((slots // 2,)),
             dma((slots,)),
-            dma((slots,)),
+            dma((slots // 2,)),
+            dma((slots // 2,)),
             dma((n,)),
             dma((n,)),
+            dma((1,)),
+            dma((2,)),
+            dma((2,)),
+            dma((1,)),
             dma((8,)),
             dma((8,)),
         ],

time: 67.9 us -> 59.2 us (0.87)
  the two profiles are of different devices: /device:TPU:9 before, /device:TPU:5 now
where the time goes in v3:
time: 59.2 us; the launch traced here: 59 us
  Pallas kernels  53.8 us (91%)
  local copies, waits for them, and re-layouts  4.52 us (8%)
  between operations  0.64 us (1%)
    pallas_call x1, Pallas kernels, body(): pl.pallas_call(functools.partial(kernel, rows, n), out_shape=[jax.ShapeDt...  53.8 us
    unnamed x2, local copies, waits for them, and re-layouts  4.52 us

profile of v3, /device:TPU:5, one launch (start us, length us, event | category | flops | bytes accessed | tf_op | source)
XLA Modules:
  0.0 59.0 jit_solution(16157795838110229671)
XLA Ops:
  0.6 53.8 %coadd.1 = (f32[512,512]{1,0:T(8,128)}, f32[512,512]{1,0:T(8,128)}) custom-call(s32[1,8]{1,0:T(1,128)} %slot_row.1, s32[2,1,16]{2,1,0:T(1,128)} %offs.1, s32[1,8]{1,0:T(1,128)} %slot_row.1, bf16[1,8]{1,0:T(2,128)(2,1)} %weight_row.1, bf16[8,256,256]{2,1,0:T(8,128)(2,1)} %bitcast.3, bf16[8,5,256,256]{3,2,1,0:T(8,128)(2,1)} %bitcast.2, ...), custom_call_target="tpu_custom_call" | custom-call | tf_op jit(solution)/shard_map/coadd/pallas_call | solution.py:442
  54.5 2.3 %copy.11 = f32[512,512]{1,0:T(8,128)} copy(f32[512,512]{1,0:T(8,128)} %get-tuple-element.4) | data formatting | bytes 2097152
  56.7 2.3 %copy.12 = f32[512,512]{1,0:T(8,128)} copy(f32[512,512]{1,0:T(8,128)} %get-tuple-element.5) | data formatting | bytes 2097152

commit v4 on v3

--- a/solution.py
+++ b/solution.py
@@ -58,10 +58,10 @@
     rows, n,
     slot_at, offs, slot_row, weight_row,
     tiles_hbm, coeffs_hbm, basis_hbm, bands_hbm,
-    coadd_hbm, detect_hbm,
+    coadd_hbm, vert_hbm, sides_hbm, ends_hbm,
     tiles, coeffs, basis, bands, send_far, recv_far, send_near, recv_near, wsend, wrecv,
     osend, orecv, numer, inverse, result, part_out, part_in, rowcov, colcov,
-    cb, vhalo, hsend, hhalo, corner, local_sem,
+    cb, vhalo, hsend, hhalo, corner, vert_out, sides_out, ends_out, local_sem,
     far_send_sem, far_recv_sem, near_send_sem, near_recv_sem, wsend_sem, wrecv_sem,
     osend_sem, orecv_sem, part_send_sem, part_recv_sem, hsend_sem, hrecv_sem,
 ):
@@ -79,7 +79,6 @@
     load_coeffs.start()
     load_bands.start()
     gmid = bands.at[pl.ds(0, patch), :]
-    gcorner = bands.at[pl.ds(patch, 2 * LANES), :]
     gedge = bands.at[pl.ds(patch + 2 * LANES, 2 * EDGE), :]
     pick = bands.at[pl.ds(patch + 2 * LANES + 2 * EDGE, 2 * EDGE), :]
 
@@ -407,18 +406,33 @@
         def _(move=move):
             halo_copy(move).wait_recv()
 
-    vert = (vert + dot_0(gedge[...], vhalo[...])).astype(bf16)
-    sides = dot_t(gmid[...], hhalo[...]).astype(bf16)
-    ends = dot_0(gedge[...], corner[...]).astype(bf16)
-    result[...] = dot(vert, gmid[...]) + dot(sides, gedge[...]) + dot(ends, gcorner[...])
-    store_result = pltpu.make_async_copy(result, detect_hbm, local_sem.at[3])
-    store_result.start()
+    vert_out[...] = (vert + dot_0(gedge[...], vhalo[...])).astype(bf16)
+    sides_out[...] = dot_t(gmid[...], hhalo[...]).astype(bf16)
+    ends_out[...] = dot_0(gedge[...], corner[...]).astype(bf16)
+    stores = [
+        pltpu.make_async_copy(src, dst, local_sem.at[at])
+        for src, dst, at in ((vert_out, vert_hbm, 3), (sides_out, sides_hbm, 6), (ends_out, ends_hbm, 7))
+    ]
+    for store in stores:
+        store.start()
     for move in moves:
         @pl.when(move[1])
         def _(move=move):
             halo_copy(move).wait_send()
     store_coadd.wait()
-    store_result.wait()
+    for store in stores:
+        store.wait()
+
+
+def finish(coadd_in, vert, sides, ends, bands, coadd_out, detection):
+    patch = vert.shape[1]
+    corner_end = patch + 2 * LANES
+    coadd_out[...] = coadd_in[...]
+    detection[...] = (
+        dot(vert[...], bands[:patch, :])
+        + dot(sides[...], bands[corner_end:corner_end + 2 * EDGE, :])
+        + dot(ends[...], bands[patch:corner_end, :])
+    )
 
 
 def body(rows, n, tiles, coeffs, weights, tile_slot, slot_offset):
@@ -439,11 +453,16 @@
     vmem = pl.BlockSpec(memory_space=pltpu.VMEM)
     anyspace = pl.BlockSpec(memory_space=pl.ANY)
     dma = pltpu.SemaphoreType.DMA
-    return pl.pallas_call(
+    parts = pl.pallas_call(
         functools.partial(kernel, rows, n),
-        out_shape=[jax.ShapeDtypeStruct((patch, patch), f32)] * 2,
+        out_shape=[
+            jax.ShapeDtypeStruct((patch, patch), f32),
+            jax.ShapeDtypeStruct((patch, patch), bf16),
+            jax.ShapeDtypeStruct((patch, 2 * EDGE), bf16),
+            jax.ShapeDtypeStruct((patch, 2 * LANES), bf16),
+        ],
         in_specs=[smem] * 2 + [vmem] * 2 + [anyspace] * 4,
-        out_specs=[anyspace] * 2,
+        out_specs=[anyspace] * 4,
         scratch_shapes=[
             pltpu.VMEM((count, size, size), bf16),
             pltpu.VMEM((count, NB, size, size), bf16),
@@ -469,7 +488,10 @@
             pltpu.VMEM((2 * EDGE, patch), bf16),
             pltpu.VMEM((2 * EDGE, patch), bf16),
             pltpu.VMEM((2 * EDGE, 2 * LANES), bf16),
-            dma((6,)),
+            pltpu.VMEM((patch, patch), bf16),
+            pltpu.VMEM((patch, 2 * EDGE), bf16),
+            pltpu.VMEM((patch, 2 * LANES), bf16),
+            dma((8,)),
             dma((slots // 2,)),
             dma((slots,)),
             dma((slots // 2,)),
@@ -490,6 +512,21 @@
     )(
         tile_slot, slot_offset, tile_slot, weights, tiles[0], coeffs[0], basis, bands,
     )
+    strip = patch // 2
+
+    def strips(columns):
+        return pl.BlockSpec((strip, columns), lambda i: (i, 0))
+
+    return tuple(pl.pallas_call(
+        finish,
+        grid=(patch // strip,),
+        out_shape=[jax.ShapeDtypeStruct((patch, patch), f32)] * 2,
+        in_specs=[strips(patch), strips(patch), strips(2 * EDGE), strips(2 * LANES),
+                  pl.BlockSpec(bands_np.shape, lambda i: (0, 0))],
+        out_specs=[strips(patch)] * 2,
+        compiler_params=pltpu.CompilerParams(vmem_limit_bytes=VMEM_LIMIT),
+        name="finish",
+    )(*parts, bands))
 
 
 def solution(mesh):

time: 59.2 us -> 57.1 us (0.965)
  local copies, waits for them, and re-layouts: 4.52 us -> 0 us
  Pallas kernels: 53.8 us -> 56.3 us
    unnamed x2 -> x0, local copies, waits for them, and re-layouts: 4.52 us -> none
    pallas_call x0 -> x1, Pallas kernels: none -> 3.27 us  [body(): pl.pallas_call(finish, grid=(patch // strip,), out_shape=[jax.ShapeDtypeS...]
    pallas_call x1, Pallas kernels: 53.8 us -> 53 us  [body(): pl.pallas_call(functools.partial(kernel, rows, n), out_shape=[jax.ShapeDt...]
where the time goes in v4:
time: 57.1 us; the launch traced here: 56.9 us
  Pallas kernels  56.3 us (99%)
  between operations  0.64 us (1%)
    pallas_call x1, Pallas kernels, body(): pl.pallas_call(functools.partial(kernel, rows, n), out_shape=[jax.ShapeDt...  53 us
    pallas_call x1, Pallas kernels, body(): pl.pallas_call(finish, grid=(patch // strip,), out_shape=[jax.ShapeDtypeS...  3.27 us

profile of v4, /device:TPU:5, one launch (start us, length us, event | category | flops | bytes accessed | tf_op | source)
XLA Modules:
  0.0 56.9 jit_solution(4923882292057782298)
XLA Ops:
  0.6 53.0 %coadd.1 = (f32[512,512]{1,0:T(8,128)}, bf16[512,512]{1,0:T(8,128)(2,1)}, bf16[512,32]{1,0:T(8,128)(2,1)}, bf16[512,256]{1,0:T(8,128)(2,1)}) custom-call(s32[1,8]{1,0:T(1,128)} %slot_row.1, s32[2,1,16]{2,1,0:T(1,128)} %offs.1, s32[1,8]{1,0:T(1,128)} %slot_row.1, bf16[1,8]{1,0:T(2,128)(2,1)} %weight_row.1, bf16[8,256,256]{2,1,0:T(8,128)(2,1)} %bitcast.3, ...), custom_call_target="tpu_custom_call" | custom-call | tf_op jit(solution)/shard_map/coadd/pallas_call | solution.py:456
  53.7 3.3 %finish.1 = (f32[512,512]{1,0:T(8,128)}, f32[512,512]{1,0:T(8,128)}) custom-call(f32[512,512]{1,0:T(8,128)} %get-tuple-element.6.coadd_in, bf16[512,512]{1,0:T(8,128)(2,1)} %get-tuple-element.7.vert, bf16[512,32]{1,0:T(8,128)(2,1)} %get-tuple-element.8.sides, bf16[512,256]{1,0:T(8,128)(2,1)} %get-tuple-element.9.ends, ...), custom_call_target="tpu_custom_call" | custom-call | tf_op jit(solution)/shard_map/finish/pallas_call | solution.py:520
